TPU v7x, 32 devices: a whole 2x2x4 slice. The times are simulated.
32 devices in a mesh: vocab: 8 (over z, y), seq: 4 (over x, core).
Axes of the slice: x: 2, y: 2, z: 4, core: 2. Of those that a mesh axis runs over, the one named last changes fastest.
Arguments:
- hidden: bfloat16 [512, 3584], P('seq', 'vocab'), may hold values from -16 to 16, as said below
- weight: bfloat16 [32000, 3584], P(('vocab', 'seq')), may hold values from -1 to 1, as said below
- targets: int32 [512], P('seq'), may hold values from 0 to 31999
- loss_mask: int32 [512], P('seq'), may hold values from 0 to 1, as said below
Outputs:
- lse: float32 [512], P('seq')
- token_loss: float32 [512], P('seq')
- ce_mean: float32 [], replicated
- z_root: float32 [], replicated
Inputs may be any that keep to these rules, and one draw needn't show every extreme that they name: Each token's hidden state, of order one. `weight`: rows of order one over the square root of 3584. `loss_mask`: at least one token is counted.
All inputs are finite; a program needn't handle non-finite values.
Results may differ from a plain program's by a relative error of at most 0.0003.
Values may be sent and summed in bfloat16 or wider, within the bound.
A program may use at most 64 MiB of HBM per device.

v0:
```python
import jax
import jax.numpy as jnp
from jax import lax
from jax.sharding import PartitionSpec as P


def on_device(hidden, weight, targets, loss_mask):
    voc_local = weight.shape[0]
    tok_local = targets.shape[0]
    all_ids, all_keep = (
        lax.all_gather(targets, "seq", axis=0, tiled=True),
        lax.all_gather(loss_mask, "seq", axis=0, tiled=True),
    )
    col_set = lax.all_gather(hidden, "vocab", axis=1, tiled=True)
    logits = lax.dot_general(
        lax.all_gather(col_set, "seq", axis=0, tiled=True),
        weight,
        (((1,), (1,)), ((), ())),
        preferred_element_type=jnp.float32,
    )
    block_index = lax.axis_index("vocab") * lax.axis_size("seq") + lax.axis_index("seq")
    columns = block_index * voc_local + jnp.arange(voc_local, dtype=jnp.int32)
    target_hit = columns[None, :] == all_ids[:, None]
    target_part = jnp.sum(jnp.where(target_hit, logits, jnp.float32(0.0)), axis=1)
    local_peak = jnp.max(logits, axis=1)
    own_start = lax.axis_index("seq") * tok_local
    row_peak = lax.pmax(local_peak, ("vocab", "seq"))
    exp_part = jnp.sum(jnp.exp(logits - row_peak[:, None]), axis=1)
    share_exp, share_target = (
        lax.psum_scatter(exp_part, "seq", scatter_dimension=0, tiled=True),
        lax.psum_scatter(target_part, "seq", scatter_dimension=0, tiled=True),
    )
    exp_total, target_logit = lax.psum((share_exp, share_target), "vocab")
    own_peak = lax.dynamic_slice_in_dim(row_peak, own_start, tok_local, 0)
    lse = own_peak + jnp.log(exp_total)
    keep = loss_mask.astype(jnp.float32)
    token_loss = keep * (lse - target_logit)
    loss_sum, square_sum, count = lax.psum(
        (jnp.sum(token_loss), jnp.sum(keep * lse * lse), jnp.sum(keep)), "seq"
    )
    ce_mean = loss_sum / count
    z_root = jnp.sqrt(square_sum / count)
    return (lse, token_loss, ce_mean, z_root)


def solution(mesh):
    in_specs = (P("seq", "vocab"), P(("vocab", "seq"), None), P("seq"), P("seq"))
    out_specs = (P("seq"), P("seq"), P(), P())
    return jax.shard_map(
        on_device, mesh=mesh, in_specs=in_specs, out_specs=out_specs, check_vma=False
    )
```

profile of v0, /device:TPU:0, one launch (start us, length us, event | category | flops | bytes accessed | tf_op | source)
XLA Modules:
  0.0 170.8 jit_solution(12204780410782226606)
XLA Ops:
  7.2 0.0 all-gather.3.cloned.1.call-start
  7.2 36.4 %all_gather.9 = bf16[128,3584]{0,1:T(8,128)(2,1)} all-gather(bf16[128,448]{0,1:T(8,128)(2,1)} %param.4), channel_id=1, replica_groups=mesh['vocab'=8,'seq'=4] {'vocab'}, dimensions={1}, use_global_device_ids=true | all-gather | bytes 1032192 | tf_op jit(solution)/shard_map/all_gather | solution.py:14
  43.6 0.0 all-gather.3.cloned.1.call-update
  43.6 1.2 dynamic-slice
  45.5 5.2 %all-gather = s32[4,1,128]{2,1,0:T(1,128)S(1)} all-gather(s32[1,1,128]{2,1,0:T(1,128)} %bitcast.6), channel_id=1, replica_groups=mesh['vocab'=8,'seq'=4] {'seq'}, dimensions={0}, use_global_device_ids=true | all-gather | bytes 2560 | tf_op jit(solution)/shard_map/all_gather | solution.py:11
  50.7 26.2 %all-gather.3.cloned.1.call-done = bf16[512,3584]{0,1:T(8,128)(2,1)} async-done(((bf16[128,3584]{0,1:T(8,128)(2,1)}), bf16[512,3584]{0,1:T(8,128)(2,1)}) %all-gather.3.cloned.1.call-update) | async-done | bytes 3670032 | tf_op jit(solution)/shard_map/all_gather | solution.py:16
  76.9 7.3 %fusion.2 = (f32[512]{0:T(512)S(1)}, f32[512,1000]{0,1:T(8,128)S(1)}) fusion(bf16[512,3584]{0,1:T(8,128)(2,1)} %all-gather.3.cloned.1.call-done, bf16[1000,3584]{1,0:T(8,128)(2,1)} %param.5), kind=kOutput, calls=%fused_computation.9 | convolution fusion | flops 3670527488 | bytes 12888064 | tf_op jit(solution)/shard_map/dot_general | solution.py:15
  84.1 0.0 copy-start
  84.2 39.4 %pmax.7 = f32[512]{0:T(512)S(1)} all-reduce(f32[512]{0:T(512)S(1)} %get-tuple-element.18), channel_id=1, replica_groups=mesh['vocab'=8,'seq'=4] {'vocab','seq'}, use_global_device_ids=true, to_apply=%region_1.2 | all-reduce | flops 512 | bytes 4096 | tf_op jit(solution)/shard_map/pmax | solution.py:27
  123.5 0.5 select_reduce_fusion
  124.0 6.6 %all-reduce.4 = (f32[512]{0:T(512)S(1)}, f32[512]{0:T(512)S(1)}) all-reduce(f32[512]{0:T(512)S(1)} %get-tuple-element.5, f32[512]{0:T(512)S(1)} %get-tuple-element.4), channel_id=2, replica_groups=mesh['vocab'=8,'seq'=4] {'seq'}, use_global_device_ids=true, to_apply=%region_3.4.clone | all-reduce | flops 1024 | bytes 8192
  130.6 0.1 dynamic-slice.1
  130.7 0.1 dynamic-slice.3
  130.7 20.1 %all-reduce.2 = (f32[128]{0:T(128)S(1)}, f32[128]{0:T(128)S(1)}) all-reduce(f32[128]{0:T(128)S(1)} %dynamic-slice.1, f32[128]{0:T(128)S(1)} %dynamic-slice.3), channel_id=1, replica_groups=mesh['vocab'=8,'seq'=4] {'vocab'}, use_global_device_ids=true, to_apply=%region_4.5 | all-reduce | flops 256 | bytes 2048 | tf_op jit(solution)/shard_map/psum | solution.py:33
  150.9 0.0 copy-done
  150.9 0.7 fusion
  151.6 0.0 copy-start.1
  151.6 1.2 fusion.1
  152.8 6.3 %all-reduce.3 = (f32[]{:T(128)}, f32[]{:T(128)}, f32[]{:T(128)}) all-reduce(f32[]{:T(128)} %get-tuple-element.16, f32[]{:T(128)} %get-tuple-element.7, f32[]{:T(128)} %get-tuple-element.6), channel_id=1, replica_groups=mesh['vocab'=8,'seq'=4] {'seq'}, use_global_device_ids=true, to_apply=%region_9.10 | all-reduce | flops 3 | bytes 24 | tf_op jit(solution)/shard_map/psum | solution.py:38
  161.6 0.0 copy-done.1
  (1 shorter events, 0.0 us)
Async XLA Ops:
  7.2 69.7 %all-gather.3.cloned.1.call-start = ((), (), s32[]{:S(2)}) async-start(), calls=%async_computation | async-start | bytes 4587520 | tf_op jit(solution)/shard_map/all_gather | solution.py:16
  84.1 66.7 %copy-start = (s32[128]{0:T(128)S(1)}, s32[128]{0:T(128)}, u32[]{:S(2)}) copy-start(s32[128]{0:T(128)} %param.7) | copy-start | bytes 1540
  151.6 10.1 %copy-start.1 = (f32[128]{0:T(128)}, f32[128]{0:T(128)S(1)}, u32[]{:S(2)}) copy-start(f32[128]{0:T(128)S(1)} %get-tuple-element.15) | copy-start | bytes 1540
Sparse Core Ops, SparseCore 0:
  43.7 33.1 all-gather.2
where the time goes:
time: 171 us
  blocking collectives  114 us (67%)
  waiting for transfers between devices  26.2 us (15%)
  between operations  19.6 us (11%)
  matrix products  7.26 us (4%)
  other arithmetic  2.37 us (1%)
    pmax x1, blocking collectives, on_device(): row_peak = lax.pmax(local_peak, ('vocab', 'seq'))  39.4 us
    all_gather x1, blocking collectives, on_device(): col_set = lax.all_gather(hidden, 'vocab', axis=1, tiled=True)  36.4 us
    all_gather x1, waiting for transfers between devices, on_device(): lax.all_gather(col_set, 'seq', axis=0, tiled=True)  26.2 us
    psum x1, blocking collectives, on_device(): exp_total, target_logit = lax.psum((share_exp, share_target), 'vocab')  20.1 us
    dot_general x1, matrix products, on_device(): lax.dot_general(lax.all_gather(col_set, 'seq', axis=0, tiled=True), weigh...  7.26 us
    unnamed x1, blocking collectives  6.59 us
    psum x1, blocking collectives, on_device(): lax.psum((jnp.sum(token_loss), jnp.sum(keep * lse * lse), jnp.sum(keep)),...  6.3 us
    all_gather x1, blocking collectives, on_device(): lax.all_gather(targets, 'seq', axis=0, tiled=True)  5.18 us
  transfers between devices with their start and end apart: 1, of which 1 were waited for; matrix products, arithmetic and copies ran while one was open for 1% of the time, Pallas kernels for 0%

commit v1 on v0

v1 whole, which is shorter than its diff:
```python
import functools
import jax
import jax.numpy as jnp
from jax import lax
from jax.experimental import pallas as pl
from jax.experimental.pallas import tpu as pltpu
from jax.sharding import PartitionSpec as P

MESH = pl.DeviceIdType.MESH
LANES = 128


def general(hidden, weight, targets, loss_mask):
    voc_local = weight.shape[0]
    all_ids = lax.all_gather(targets, "seq", axis=0, tiled=True)
    hidden = lax.all_gather(hidden, "vocab", axis=1, tiled=True)
    logits = lax.dot_general(
        lax.all_gather(hidden, "seq", axis=0, tiled=True),
        weight,
        (((1,), (1,)), ((), ())),
        preferred_element_type=jnp.float32,
    )
    block_index = lax.axis_index("vocab") * lax.axis_size("seq") + lax.axis_index("seq")
    columns = block_index * voc_local + jnp.arange(voc_local, dtype=jnp.int32)
    target_hit = columns[None, :] == all_ids[:, None]
    target_part = jnp.sum(jnp.where(target_hit, logits, jnp.float32(0.0)), axis=1)
    row_peak = lax.pmax(jnp.max(logits, axis=1), ("vocab", "seq"))
    exp_part = jnp.sum(jnp.exp(logits - row_peak[:, None]), axis=1)
    share_exp, share_target = (
        lax.psum_scatter(exp_part, "seq", scatter_dimension=0, tiled=True),
        lax.psum_scatter(target_part, "seq", scatter_dimension=0, tiled=True),
    )
    exp_total, target_logit = lax.psum((share_exp, share_target), "vocab")
    tok_local = targets.shape[0]
    own_peak = lax.dynamic_slice_in_dim(row_peak, lax.axis_index("seq") * tok_local, tok_local, 0)
    lse = own_peak + jnp.log(exp_total)
    keep = loss_mask.astype(jnp.float32)
    token_loss = keep * (lse - target_logit)
    loss_sum, square_sum, count = lax.psum(
        (jnp.sum(token_loss), jnp.sum(keep * lse * lse), jnp.sum(keep)), "seq"
    )
    return (lse, token_loss, loss_sum / count, jnp.sqrt(square_sum / count))


def kernel(
    n_voc, n_seq,
    h_ref, w_hbm, tgt_ref, msk_ref,
    lse_ref, tl_ref, ce_ref, zr_ref,
    G, W, acc, meta, part,
    w_sem, recv, up_sem, down_sem, p_sem, q_sem, sib_sem, meta_send, meta_recv, part_send, part_recv,
):
    Z = n_voc // 2
    n_dev = n_voc * n_seq
    v, s = lax.axis_index("vocab"), lax.axis_index("seq")
    z, y, x, c = v // 2, v % 2, s // 2, s % 2
    me = v * n_seq + s
    voc, toks = w_hbm.shape[0], h_ref.shape[0]
    feat = h_ref.shape[1]
    full = feat // LANES
    half = toks // 2

    load = pltpu.make_async_copy(w_hbm, W, w_sem)
    load.start()

    barrier = pltpu.get_barrier_semaphore()

    def greet(i, carry):
        d = lax.rem(me + i, n_dev)
        pl.semaphore_signal(barrier, inc=1, device_id=(d // n_seq, d % n_seq), device_id_type=MESH)
        return carry

    lax.fori_loop(1, n_dev, greet, 0)

    @pl.when(y == 0)
    def _():
        for j in range(full):
            G[me, j * toks:(j + 1) * toks, :] = h_ref[:, j * LANES:(j + 1) * LANES]
        odd = h_ref[:, full * LANES:feat]
        G[me, full * toks:full * toks + half, :] = jnp.concatenate([odd[:half], odd[half:]], axis=1)

    @pl.when(y == 1)
    def _():
        lead = feat - full * LANES
        for j in range(full):
            G[me, j * toks:(j + 1) * toks, :] = h_ref[:, lead + j * LANES:lead + (j + 1) * LANES]
        odd = h_ref[:, :lead]
        G[me, full * toks:full * toks + half, :] = jnp.concatenate([odd[half:], odd[:half]], axis=1)

    meta[s, 0:1, :] = tgt_ref[...]
    meta[s, 1:2, :] = msk_ref[...]

    pl.semaphore_wait(barrier, n_dev - 1)

    flip_y, flip_x = 1 - 2 * y, 2 - 4 * x
    sib = s + 1 - 2 * c
    p_v, p_s = v + (1 - c) * flip_y, s + c * flip_x
    q_v, q_s = v + c * flip_y, s + (1 - c) * flip_x

    def block(zz, yy, ss):
        return (2 * zz + yy) * n_seq + ss

    def push(b, sem, dv, ds):
        pltpu.make_async_remote_copy(
            src_ref=G.at[b], dst_ref=G.at[b], send_sem=sem, recv_sem=recv.at[b],
            device_id=(dv, ds), device_id_type=MESH,
        ).start()

    def arrived(b):
        pltpu.make_async_remote_copy(
            src_ref=G.at[b], dst_ref=G.at[b], send_sem=sib_sem, recv_sem=recv.at[b],
            device_id=(v, sib), device_id_type=MESH,
        ).wait_recv()

    near = jnp.minimum(z, Z - 1 - z)
    far_side = jnp.where(2 * z < Z, 1, -1)

    def order(i):
        in_near = i <= 2 * near
        sgn = jnp.where(in_near, jnp.where(i % 2 == 1, -1, 1), far_side)
        dist = jnp.where(in_near, (i + 1) // 2, i - near)
        return z + sgn * dist

    def to_sib(b):
        push(b, sib_sem, v, sib)

    def line(zz):
        b = block(zz, y, s)

        @pl.when(jnp.logical_and(zz <= z, z + 1 < Z))
        def _():
            push(b, up_sem.at[zz], v + 2, s)

        @pl.when(jnp.logical_and(zz >= z, z > 0))
        def _():
            push(b, down_sem.at[zz], v - 2, s)

        push(b, p_sem, p_v, p_s)
        push(b, q_sem, q_v, q_s)
        to_sib(b)

    line(z)

    def tell(i, carry):
        d = lax.rem(s + i, n_seq)
        pltpu.make_async_remote_copy(
            src_ref=meta.at[s], dst_ref=meta.at[s], send_sem=meta_send, recv_sem=meta_recv,
            device_id=(v, d), device_id_type=MESH,
        ).start()
        return carry

    lax.fori_loop(1, n_seq, tell, 0)

    p_y, q_y = p_v % 2, q_v % 2

    def from_p(zz):
        b = block(zz, p_y, p_s)
        arrived(b)
        to_sib(b)

    def from_q(zz):
        b = block(zz, q_y, q_s)
        arrived(b)
        to_sib(b)

    def phase1(i, carry):
        zz = order(i)
        arrived(block(zz, y, s))
        line(zz)
        from_p(order(i - 1))

        @pl.when(i >= 2)
        def _():
            from_q(order(i - 2))

        return carry

    lax.fori_loop(1, Z, phase1, 0)

    def on_to_q(zz):
        push(block(zz, p_y, p_s), q_sem, q_v, q_s)

    def early_q(i, carry):
        on_to_q(order(i))
        return carry

    lax.fori_loop(0, Z - 1, early_q, 0)
    from_p(order(Z - 1))
    on_to_q(order(Z - 1))

    def late_q(i, carry):
        from_q(order(i))
        return carry

    lax.fori_loop(max(Z - 2, 0), Z, late_q, 0)

    low = lax.broadcasted_iota(jnp.int32, (half, LANES), 1) < LANES // 2

    def chunk(zz, xx, first):
        sides = []
        for cc in range(2):
            b0, b1 = block(zz, 0, 2 * xx + cc), block(zz, 1, 2 * xx + cc)
            o0 = G[b0, full * toks:full * toks + half, :]
            o1 = G[b1, full * toks:full * toks + half, :]
            top = jnp.where(low, o0, o1)
            turned = jnp.where(low, o1, o0)
            bottom = jnp.concatenate([turned[:, LANES // 2:], turned[:, :LANES // 2]], axis=1)
            tiles = [G[b0, j * toks:(j + 1) * toks, :] for j in range(full)]
            tiles.append(jnp.concatenate([top, bottom], axis=0))
            tiles += [G[b1, j * toks:(j + 1) * toks, :] for j in range(full)]
            sides.append(jnp.concatenate(tiles, axis=1))
        rows = jnp.concatenate(sides, axis=0)
        cols = pl.ds(pl.multiple_of(zz * 2 * feat, LANES), 2 * feat)
        out = lax.dot_general(
            W[:, cols], rows, (((1,), (1,)), ((), ())), preferred_element_type=jnp.float32
        )

        @pl.when(first)
        def _():
            acc[xx] = out

        @pl.when(jnp.logical_not(first))
        def _():
            acc[xx] += out

    step = max(r for r in range(8, 257, 8) if voc % r == 0)

    def finish(xx):
        ids = jnp.concatenate([meta[2 * xx, 0:1, :], meta[2 * xx + 1, 0:1, :]], axis=1)
        ids = ids - me * voc
        wide = (8, 2 * toks)

        def peak(r, m):
            tile = acc[xx, pl.ds(pl.multiple_of(r * step, 8), step), :]
            return jnp.maximum(m, jnp.max(tile.reshape(step // 8, 8, 2 * toks), axis=0))

        m = lax.fori_loop(0, voc // step, peak, jnp.full(wide, -jnp.inf, jnp.float32))
        m = jnp.max(m, axis=0, keepdims=True)

        def total(r, carry):
            e, t = carry
            tile = acc[xx, pl.ds(pl.multiple_of(r * step, 8), step), :]
            row = lax.broadcasted_iota(jnp.int32, (step, 2 * toks), 0) + r * step
            hit = jnp.where(row == ids, tile, jnp.float32(0.0))
            e += jnp.sum(jnp.exp(tile - m).reshape(step // 8, 8, 2 * toks), axis=0)
            t += jnp.sum(hit.reshape(step // 8, 8, 2 * toks), axis=0)
            return e, t

        zero = jnp.zeros(wide, jnp.float32)
        e, t = lax.fori_loop(0, voc // step, total, (zero, zero))
        lse = m + jnp.log(jnp.sum(e, axis=0, keepdims=True))
        t = jnp.sum(t, axis=0, keepdims=True)
        for cc in range(2):
            cut = slice(cc * toks, (cc + 1) * toks)
            part[me, pl.ds(2 * xx + cc, 1), :] = lse[:, cut]
            part[me, pl.ds(n_seq + 2 * xx + cc, 1), :] = t[:, cut]

    load.wait()

    def near_chunk(i, carry):
        zz = order(i)
        arrived(block(zz, y, sib))
        arrived(block(zz, 1 - y, sib))
        chunk(zz, x, i == 0)
        return carry

    lax.fori_loop(0, Z, near_chunk, 0)

    pltpu.make_async_copy(meta.at[0:n_seq - 1], meta.at[0:n_seq - 1], meta_recv).wait()

    def far_chunk(i, carry):
        zz = order(i)
        b = block(zz, 1 - y, s + flip_x)
        arrived(b)
        to_sib(b)

        @pl.when(i == 0)
        def _():
            finish(x)

        arrived(block(zz, y, sib + flip_x))
        arrived(block(zz, 1 - y, sib + flip_x))
        chunk(zz, 1 - x, i == 0)
        return carry

    lax.fori_loop(0, Z, far_chunk, 0)
    finish(1 - x)

    def share(i, carry):
        d = lax.rem(me + i, n_dev)
        pltpu.make_async_remote_copy(
            src_ref=part.at[me], dst_ref=part.at[me], send_sem=part_send, recv_sem=part_recv,
            device_id=(d // n_seq, d % n_seq), device_id_type=MESH,
        ).start()
        return carry

    lax.fori_loop(1, n_dev, share, 0)

    def drain(zz, carry):
        @pl.when(jnp.logical_and(zz <= z, z + 1 < Z))
        def _():
            pltpu.make_async_copy(G.at[0], G.at[0], up_sem.at[zz]).wait()

        @pl.when(jnp.logical_and(zz >= z, z > 0))
        def _():
            pltpu.make_async_copy(G.at[0], G.at[0], down_sem.at[zz]).wait()

        return carry

    lax.fori_loop(0, Z, drain, 0)
    for sem, count in ((p_sem, Z), (q_sem, 2 * Z), (sib_sem, 4 * Z)):
        pltpu.make_async_copy(G.at[0:count], G.at[0:count], sem).wait()
    pltpu.make_async_copy(meta.at[0:n_seq - 1], meta.at[0:n_seq - 1], meta_send).wait()
    pltpu.make_async_copy(part.at[0:n_dev - 1], part.at[0:n_dev - 1], part_recv).wait()

    parts = part[...]
    lses, t = parts[:, :n_seq, :], jnp.sum(parts[:, n_seq:2 * n_seq, :], axis=0)
    top = jnp.max(lses, axis=0)
    lse = top + jnp.log(jnp.sum(jnp.exp(lses - top[None]), axis=0))
    keep = jnp.concatenate([meta[i, 1:2, :] for i in range(n_seq)], axis=0).astype(jnp.float32)
    loss = keep * (lse - t)

    def whole(a):
        return jnp.sum(jnp.sum(a, axis=0, keepdims=True), axis=1, keepdims=True)

    count = whole(keep)
    ce_ref[...] = whole(loss) / count
    zr_ref[...] = jnp.sqrt(whole(keep * lse * lse) / count)
    mine = lax.broadcasted_iota(jnp.int32, (n_seq, toks), 0) == s
    lse_ref[...] = jnp.sum(jnp.where(mine, lse, 0.0), axis=0, keepdims=True)
    tl_ref[...] = jnp.sum(jnp.where(mine, loss, 0.0), axis=0, keepdims=True)
    pltpu.make_async_copy(part.at[0:n_dev - 1], part.at[0:n_dev - 1], part_send).wait()


def on_device(n_voc, n_seq, hidden, weight, targets, loss_mask):
    toks, feat = hidden.shape
    voc, wide = weight.shape
    fits = (
        n_seq == 4 and n_voc % 2 == 0 and toks == LANES
        and feat % LANES == LANES // 2 and voc % 8 == 0
    )
    if not fits:
        return general(hidden, weight, targets, loss_mask)
    n_dev = n_voc * n_seq
    n_z = n_voc // 2
    f32 = jnp.float32
    dma = pltpu.SemaphoreType.DMA
    vmem = pl.BlockSpec(memory_space=pltpu.VMEM)
    lse, loss, ce, root = pl.pallas_call(
        functools.partial(kernel, n_voc, n_seq),
        out_shape=(
            jax.ShapeDtypeStruct((1, toks), f32),
            jax.ShapeDtypeStruct((1, toks), f32),
            jax.ShapeDtypeStruct((1, 1), f32),
            jax.ShapeDtypeStruct((1, 1), f32),
        ),
        in_specs=[vmem, pl.BlockSpec(memory_space=pl.ANY), vmem, vmem],
        out_specs=(vmem, vmem, vmem, vmem),
        scratch_shapes=[
            pltpu.VMEM((n_dev, toks * feat // LANES, LANES), jnp.bfloat16),
            pltpu.VMEM((voc, wide), jnp.bfloat16),
            pltpu.VMEM((2, voc, 2 * toks), f32),
            pltpu.VMEM((n_seq, 8, LANES), jnp.int32),
            pltpu.VMEM((n_dev, 2 * n_seq, LANES), f32),
            dma, dma((n_dev,)), dma((n_z,)), dma((n_z,)),
            dma, dma, dma, dma, dma, dma, dma,
        ],
        compiler_params=pltpu.CompilerParams(
            collective_id=0, has_side_effects=True, vmem_limit_bytes=48 * 2**20
        ),
        cost_estimate=pl.CostEstimate(
            flops=2 * n_seq * toks * wide * voc, bytes_accessed=2 * voc * wide,
            transcendentals=n_seq * toks * voc,
        ),
    )(hidden, weight, targets.reshape(1, toks), loss_mask.reshape(1, toks))
    return (lse.reshape(toks), loss.reshape(toks), ce.reshape(()), root.reshape(()))


def solution(mesh):
    in_specs = (P("seq", "vocab"), P(("vocab", "seq"), None), P("seq"), P("seq"))
    out_specs = (P("seq"), P("seq"), P(), P())
    return jax.shard_map(
        functools.partial(on_device, mesh.shape["vocab"], mesh.shape["seq"]),
        mesh=mesh, in_specs=in_specs, out_specs=out_specs, check_vma=False,
    )
```

time: 171 us -> 48.8 us (0.29)
  blocking collectives: 114 us -> 0 us
  Pallas kernels: 0 us -> 41.1 us
  waiting for transfers between devices: 26.2 us -> 0 us
  between operations: 19.6 us -> 4.15 us
  matrix products: 7.26 us -> 0 us
  other arithmetic: 2.37 us -> 0 us
  local copies, waits for them, and re-layouts: 1.4 us -> 3.33 us
    all_gather x2 -> x0, blocking collectives: 41.5 us -> none  [the longest x1 36.4 us: on_device(): col_set = lax.all_gather(hidden, 'vocab', axis=1, tiled=True)]
    pallas_call x0 -> x1, Pallas kernels: none -> 41.1 us  [on_device(): pl.pallas_call(functools.partial(kernel, n_voc, n_seq), out_shape=(jax.Sh...]
    pmax x1 -> x0, blocking collectives: 39.4 us -> none  [on_device(): row_peak = lax.pmax(local_peak, ('vocab', 'seq'))]
    psum x2 -> x0, blocking collectives: 26.4 us -> none  [the longest x1 20.1 us: on_device(): exp_total, target_logit = lax.psum((share_exp, share_target), 'vocab')]
    all_gather x1 -> x0, waiting for transfers between devices: 26.2 us -> none  [on_device(): lax.all_gather(col_set, 'seq', axis=0, tiled=True)]
    dot_general x1 -> x0, matrix products: 7.26 us -> none  [on_device(): lax.dot_general(lax.all_gather(col_set, 'seq', axis=0, tiled=True), weigh...]
    unnamed x1 -> x0, blocking collectives: 6.59 us -> none
    reduce_sum x3 -> x0, other arithmetic: 2.36 us -> none  [the longest x1 1.19 us: on_device(): jnp.sum(token_loss)]
  transfers between devices with their start and end apart: 1 -> 0, of which waited for: 1 -> 0; matrix products, arithmetic and copies ran while one was open for 1% -> 0% of each run, Pallas kernels for 0% -> 0%
where the time goes in v1:
time: 48.8 us; the launch traced here: 48.6 us
  Pallas kernels  41.1 us (84%)
  between operations  4.15 us (9%)
  local copies, waits for them, and re-layouts  3.33 us (7%)
    pallas_call x1, Pallas kernels, on_device(): pl.pallas_call(functools.partial(kernel, n_voc, n_seq), out_shape=(jax.Sh...  41.1 us
    unnamed x7, local copies, waits for them, and re-layouts  3.33 us

profile of v1, /device:TPU:0, one launch (start us, length us, event | category | flops | bytes accessed | tf_op | source)
XLA Modules:
  0.0 48.6 jit_solution(16007180790325321473)
XLA Ops:
  0.6 1.0 %copy.8.h_ref = bf16[128,448]{1,0:T(8,128)(2,1)S(1)} copy(bf16[128,448]{0,1:T(8,128)(2,1)} %param.4) | data formatting | bytes 229376 | tf_op args[0]
  1.6 0.0 copy-start
  1.6 0.6 %copy-done = s32[128]{0:T(128)S(1)} copy-done((s32[128]{0:T(128)S(1)}, s32[128]{0:T(128)}, u32[]{:S(2)}) %copy-start) | copy-done | bytes 536
  2.3 0.0 copy-start.1
  2.3 0.7 %copy-done.1 = s32[128]{0:T(128)S(1)} copy-done((s32[128]{0:T(128)S(1)}, s32[128]{0:T(128)}, u32[]{:S(2)}) %copy-start.1) | copy-done | bytes 536
  3.0 41.1 %shard_map.75 = (f32[1,128]{1,0:T(1,128)S(1)}, f32[1,128]{1,0:T(1,128)S(1)}, f32[1,1]{1,0:T(1,128)}, f32[1,1]{1,0:T(1,128)}) custom-call(bf16[128,448]{1,0:T(8,128)(2,1)S(1)} %copy.8.h_ref, bf16[1000,3584]{1,0:T(8,128)(2,1)} %w_hbm.1, s32[1,128]{1,0:T(1,128)S(1)} %bitcast.6, s32[1,128]{1,0:T(1,128)S(1)} %bitcast.7), custom_call_target="tpu_custom_call" | custom-call | flops 3670016000 | bytes 7168000 | tf_op jit(solution)/shard_map/pallas_call | solution.py:348
  44.1 0.5 %copy.13 = f32[128]{0:T(128)} copy(f32[128]{0:T(128)S(1)} %bitcast.9) | data formatting | bytes 1024
  44.6 0.5 %copy.14 = f32[128]{0:T(128)} copy(f32[128]{0:T(128)S(1)} %bitcast.8) | data formatting | bytes 1024
Async XLA Ops:
  1.6 0.7 %copy-start = (s32[128]{0:T(128)S(1)}, s32[128]{0:T(128)}, u32[]{:S(2)}) copy-start(s32[128]{0:T(128)} %param.6) | copy-start | bytes 1540
  2.3 0.7 %copy-start.1 = (s32[128]{0:T(128)S(1)}, s32[128]{0:T(128)}, u32[]{:S(2)}) copy-start(s32[128]{0:T(128)} %param.7) | copy-start | bytes 1540

commit v2 on v1

--- a/solution.py
+++ b/solution.py
@@ -46,19 +46,24 @@
     n_voc, n_seq,
     h_ref, w_hbm, tgt_ref, msk_ref,
     lse_ref, tl_ref, ce_ref, zr_ref,
-    G, W, acc, meta, part,
-    w_sem, recv, up_sem, down_sem, p_sem, q_sem, sib_sem, meta_send, meta_recv, part_send, part_recv,
+    G, W, acc, meta, part, done,
+    w_sem, in_sem, recv, up_sem, down_sem, p_sem, q_sem, sib_sem, meta_send, meta_recv, part_send, part_recv,
 ):
     Z = n_voc // 2
     n_dev = n_voc * n_seq
     v, s = lax.axis_index("vocab"), lax.axis_index("seq")
     z, y, x, c = v // 2, v % 2, s // 2, s % 2
     me = v * n_seq + s
-    voc, toks = w_hbm.shape[0], h_ref.shape[0]
-    feat = h_ref.shape[1]
-    full = feat // LANES
-    half = toks // 2
-
+    voc = w_hbm.shape[0]
+    feat, toks = h_ref.shape
+
+    own = (
+        pltpu.make_async_copy(h_ref, G.at[me], in_sem.at[0]),
+        pltpu.make_async_copy(tgt_ref, meta.at[s, pl.ds(0, 1)], in_sem.at[1]),
+        pltpu.make_async_copy(msk_ref, meta.at[s, pl.ds(1, 1)], in_sem.at[2]),
+    )
+    for copy in own:
+        copy.start()
     load = pltpu.make_async_copy(w_hbm, W, w_sem)
     load.start()
 
@@ -71,24 +76,8 @@
 
     lax.fori_loop(1, n_dev, greet, 0)
 
-    @pl.when(y == 0)
-    def _():
-        for j in range(full):
-            G[me, j * toks:(j + 1) * toks, :] = h_ref[:, j * LANES:(j + 1) * LANES]
-        odd = h_ref[:, full * LANES:feat]
-        G[me, full * toks:full * toks + half, :] = jnp.concatenate([odd[:half], odd[half:]], axis=1)
-
-    @pl.when(y == 1)
-    def _():
-        lead = feat - full * LANES
-        for j in range(full):
-            G[me, j * toks:(j + 1) * toks, :] = h_ref[:, lead + j * LANES:lead + (j + 1) * LANES]
-        odd = h_ref[:, :lead]
-        G[me, full * toks:full * toks + half, :] = jnp.concatenate([odd[half:], odd[:half]], axis=1)
-
-    meta[s, 0:1, :] = tgt_ref[...]
-    meta[s, 1:2, :] = msk_ref[...]
-
+    for copy in own:
+        copy.wait()
     pl.semaphore_wait(barrier, n_dev - 1)
 
     flip_y, flip_x = 1 - 2 * y, 2 - 4 * x
@@ -162,56 +151,15 @@
         arrived(b)
         to_sib(b)
 
-    def phase1(i, carry):
-        zz = order(i)
-        arrived(block(zz, y, s))
-        line(zz)
-        from_p(order(i - 1))
-
-        @pl.when(i >= 2)
-        def _():
-            from_q(order(i - 2))
-
-        return carry
-
-    lax.fori_loop(1, Z, phase1, 0)
-
-    def on_to_q(zz):
-        push(block(zz, p_y, p_s), q_sem, q_v, q_s)
-
-    def early_q(i, carry):
-        on_to_q(order(i))
-        return carry
-
-    lax.fori_loop(0, Z - 1, early_q, 0)
-    from_p(order(Z - 1))
-    on_to_q(order(Z - 1))
-
-    def late_q(i, carry):
-        from_q(order(i))
-        return carry
-
-    lax.fori_loop(max(Z - 2, 0), Z, late_q, 0)
-
-    low = lax.broadcasted_iota(jnp.int32, (half, LANES), 1) < LANES // 2
-
     def chunk(zz, xx, first):
         sides = []
         for cc in range(2):
-            b0, b1 = block(zz, 0, 2 * xx + cc), block(zz, 1, 2 * xx + cc)
-            o0 = G[b0, full * toks:full * toks + half, :]
-            o1 = G[b1, full * toks:full * toks + half, :]
-            top = jnp.where(low, o0, o1)
-            turned = jnp.where(low, o1, o0)
-            bottom = jnp.concatenate([turned[:, LANES // 2:], turned[:, :LANES // 2]], axis=1)
-            tiles = [G[b0, j * toks:(j + 1) * toks, :] for j in range(full)]
-            tiles.append(jnp.concatenate([top, bottom], axis=0))
-            tiles += [G[b1, j * toks:(j + 1) * toks, :] for j in range(full)]
-            sides.append(jnp.concatenate(tiles, axis=1))
-        rows = jnp.concatenate(sides, axis=0)
+            pair = [G[block(zz, yy, 2 * xx + cc)] for yy in range(2)]
+            sides.append(jnp.concatenate(pair, axis=0))
+        rows = jnp.concatenate(sides, axis=1)
         cols = pl.ds(pl.multiple_of(zz * 2 * feat, LANES), 2 * feat)
         out = lax.dot_general(
-            W[:, cols], rows, (((1,), (1,)), ((), ())), preferred_element_type=jnp.float32
+            W[:, cols], rows, (((1,), (0,)), ((), ())), preferred_element_type=jnp.float32
         )
 
         @pl.when(first)
@@ -254,35 +202,65 @@
             part[me, pl.ds(2 * xx + cc, 1), :] = lse[:, cut]
             part[me, pl.ds(n_seq + 2 * xx + cc, 1), :] = t[:, cut]
 
-    load.wait()
-
-    def near_chunk(i, carry):
+    def do_chunk(k):
+        zz, far = order(k % Z), k // Z
+        xx = x + far * (1 - 2 * x)
+        ss = 2 * xx + 1 - c
+        arrived(block(zz, 0, ss))
+        arrived(block(zz, 1, ss))
+        chunk(zz, xx, k % Z == 0)
+
+    def phase1(i, carry):
         zz = order(i)
-        arrived(block(zz, y, sib))
-        arrived(block(zz, 1 - y, sib))
-        chunk(zz, x, i == 0)
-        return carry
-
-    lax.fori_loop(0, Z, near_chunk, 0)
-
+        arrived(block(zz, y, s))
+        line(zz)
+        from_p(order(i - 1))
+
+        @pl.when(i >= 2)
+        def _():
+            from_q(order(i - 2))
+
+        @pl.when(i == 3)
+        def _():
+            load.wait()
+
+        @pl.when(i >= 3)
+        def _():
+            do_chunk(i - 3)
+
+        return carry
+
+    lax.fori_loop(1, Z, phase1, 0)
+
+    def on_to_q(zz):
+        push(block(zz, p_y, p_s), q_sem, q_v, q_s)
+
+    def early_q(i, carry):
+        on_to_q(order(i))
+        return carry
+
+    lax.fori_loop(0, Z - 1, early_q, 0)
+    from_p(order(Z - 1))
+    on_to_q(order(Z - 1))
+
+    def late_q(i, carry):
+        from_q(order(i))
+        do_chunk(i - 1)
+        return carry
+
+    lax.fori_loop(Z - 2, Z, late_q, 0)
     pltpu.make_async_copy(meta.at[0:n_seq - 1], meta.at[0:n_seq - 1], meta_recv).wait()
 
-    def far_chunk(i, carry):
-        zz = order(i)
-        b = block(zz, 1 - y, s + flip_x)
+    def last(i, carry):
+        b = block(order(i), 1 - y, s + flip_x)
         arrived(b)
         to_sib(b)
-
-        @pl.when(i == 0)
-        def _():
-            finish(x)
-
-        arrived(block(zz, y, sib + flip_x))
-        arrived(block(zz, 1 - y, sib + flip_x))
-        chunk(zz, 1 - x, i == 0)
-        return carry
-
-    lax.fori_loop(0, Z, far_chunk, 0)
+        do_chunk(Z - 1 + i)
+        return carry
+
+    lax.fori_loop(0, Z, last, 0)
+    finish(x)
+    do_chunk(2 * Z - 1)
     finish(1 - x)
 
     def share(i, carry):
@@ -326,17 +304,26 @@
     ce_ref[...] = whole(loss) / count
     zr_ref[...] = jnp.sqrt(whole(keep * lse * lse) / count)
     mine = lax.broadcasted_iota(jnp.int32, (n_seq, toks), 0) == s
-    lse_ref[...] = jnp.sum(jnp.where(mine, lse, 0.0), axis=0, keepdims=True)
-    tl_ref[...] = jnp.sum(jnp.where(mine, loss, 0.0), axis=0, keepdims=True)
+    done[0] = jnp.sum(jnp.where(mine, lse, 0.0), axis=0, keepdims=True)
+    done[1] = jnp.sum(jnp.where(mine, loss, 0.0), axis=0, keepdims=True)
+    out = (
+        pltpu.make_async_copy(done.at[0], lse_ref, in_sem.at[0]),
+        pltpu.make_async_copy(done.at[1], tl_ref, in_sem.at[1]),
+    )
+    for copy in out:
+        copy.start()
+    for copy in out:
+        copy.wait()
     pltpu.make_async_copy(part.at[0:n_dev - 1], part.at[0:n_dev - 1], part_send).wait()
 
 
 def on_device(n_voc, n_seq, hidden, weight, targets, loss_mask):
     toks, feat = hidden.shape
+    sub = 16
     voc, wide = weight.shape
     fits = (
-        n_seq == 4 and n_voc % 2 == 0 and toks == LANES
-        and feat % LANES == LANES // 2 and voc % 8 == 0
+        n_seq == 4 and n_voc % 2 == 0 and n_voc >= 8 and toks == LANES
+        and feat % sub == 0 and 2 * feat % LANES == 0 and voc % 8 == 0
     )
     if not fits:
         return general(hidden, weight, targets, loss_mask)
@@ -345,6 +332,7 @@
     f32 = jnp.float32
     dma = pltpu.SemaphoreType.DMA
     vmem = pl.BlockSpec(memory_space=pltpu.VMEM)
+    hbm = pl.BlockSpec(memory_space=pltpu.HBM)
     lse, loss, ce, root = pl.pallas_call(
         functools.partial(kernel, n_voc, n_seq),
         out_shape=(
@@ -353,25 +341,26 @@
             jax.ShapeDtypeStruct((1, 1), f32),
             jax.ShapeDtypeStruct((1, 1), f32),
         ),
-        in_specs=[vmem, pl.BlockSpec(memory_space=pl.ANY), vmem, vmem],
-        out_specs=(vmem, vmem, vmem, vmem),
+        in_specs=[hbm, hbm, hbm, hbm],
+        out_specs=(hbm, hbm, vmem, vmem),
         scratch_shapes=[
-            pltpu.VMEM((n_dev, toks * feat // LANES, LANES), jnp.bfloat16),
+            pltpu.VMEM((n_dev, feat, toks), jnp.bfloat16),
             pltpu.VMEM((voc, wide), jnp.bfloat16),
             pltpu.VMEM((2, voc, 2 * toks), f32),
             pltpu.VMEM((n_seq, 8, LANES), jnp.int32),
             pltpu.VMEM((n_dev, 2 * n_seq, LANES), f32),
-            dma, dma((n_dev,)), dma((n_z,)), dma((n_z,)),
+            pltpu.VMEM((2, 1, toks), f32),
+            dma, dma((3,)), dma((n_dev,)), dma((n_z,)), dma((n_z,)),
             dma, dma, dma, dma, dma, dma, dma,
         ],
         compiler_params=pltpu.CompilerParams(
-            collective_id=0, has_side_effects=True, vmem_limit_bytes=48 * 2**20
+            collective_id=0, has_side_effects=True, vmem_limit_bytes=64 * 2**20
         ),
         cost_estimate=pl.CostEstimate(
             flops=2 * n_seq * toks * wide * voc, bytes_accessed=2 * voc * wide,
             transcendentals=n_seq * toks * voc,
         ),
-    )(hidden, weight, targets.reshape(1, toks), loss_mask.reshape(1, toks))
+    )(hidden.T, weight, targets.reshape(1, toks), loss_mask.reshape(1, toks))
     return (lse.reshape(toks), loss.reshape(toks), ce.reshape(()), root.reshape(()))
 
 

time: 48.8 us -> 43.9 us (0.90)
  Pallas kernels: 41.1 us -> 37.3 us
  local copies, waits for them, and re-layouts: 3.33 us -> 2.25 us
    pallas_call x1, Pallas kernels: 41.1 us -> 37.3 us  [on_device(): pl.pallas_call(functools.partial(kernel, n_voc, n_seq), out_shape=(jax.Sh...]
    unnamed x7 -> x2, local copies, waits for them, and re-layouts: 3.33 us -> 2.25 us
where the time goes in v2:
time: 43.9 us; the launch traced here: 43.7 us
  Pallas kernels  37.3 us (85%)
  between operations  4.14 us (9%)
  local copies, waits for them, and re-layouts  2.25 us (5%)
    pallas_call x1, Pallas kernels, on_device(): pl.pallas_call(functools.partial(kernel, n_voc, n_seq), out_shape=(jax.Sh...  37.3 us
    unnamed x2, local copies, waits for them, and re-layouts  2.25 us

profile of v2, /device:TPU:0, one launch (start us, length us, event | category | flops | bytes accessed | tf_op | source)
XLA Modules:
  0.0 43.7 jit_solution(704382062042218592)
XLA Ops:
  0.6 37.3 %shard_map.75 = (f32[1,128]{1,0:T(1,128)}, f32[1,128]{1,0:T(1,128)}, f32[1,1]{1,0:T(1,128)}, f32[1,1]{1,0:T(1,128)}) custom-call(bf16[448,128]{1,0:T(8,128)(2,1)} %bitcast.7, bf16[1000,3584]{1,0:T(8,128)(2,1)} %w_hbm.1, s32[1,128]{1,0:T(1,128)} %bitcast.8, s32[1,128]{1,0:T(1,128)} %bitcast.9), custom_call_target="tpu_custom_call" | custom-call | flops 3670016000 | bytes 7168000 | tf_op jit(solution)/shard_map/pallas_call | solution.py:336
  38.0 1.1 %copy.12 = f32[128]{0:T(128)} copy(f32[128]{0:T(128)} %bitcast.11) | data formatting | bytes 1024
  39.1 1.1 %copy.13 = f32[128]{0:T(128)} copy(f32[128]{0:T(128)} %bitcast.10) | data formatting | bytes 1024

commit v3 on v2

--- a/solution.py
+++ b/solution.py
@@ -45,7 +45,7 @@
 def kernel(
     n_voc, n_seq,
     h_ref, w_hbm, tgt_ref, msk_ref,
-    lse_ref, tl_ref, ce_ref, zr_ref,
+    tok_ref, ce_ref, zr_ref,
     G, W, acc, meta, part, done,
     w_sem, in_sem, recv, up_sem, down_sem, p_sem, q_sem, sib_sem, meta_send, meta_recv, part_send, part_recv,
 ):
@@ -112,18 +112,26 @@
     def to_sib(b):
         push(b, sib_sem, v, sib)
 
+    def along(b, zz, side):
+        @pl.when(jnp.logical_and(zz <= z, z + 1 < Z))
+        def _():
+            push(b, up_sem.at[side, zz], v + 2, s)
+
+        @pl.when(jnp.logical_and(zz >= z, z > 0))
+        def _():
+            push(b, down_sem.at[side, zz], v - 2, s)
+
+    def is_end(zz):
+        return jnp.logical_or(zz == 0, zz == Z - 1)
+
     def line(zz):
         b = block(zz, y, s)
-
-        @pl.when(jnp.logical_and(zz <= z, z + 1 < Z))
-        def _():
-            push(b, up_sem.at[zz], v + 2, s)
-
-        @pl.when(jnp.logical_and(zz >= z, z > 0))
-        def _():
-            push(b, down_sem.at[zz], v - 2, s)
-
-        push(b, p_sem, p_v, p_s)
+        along(b, zz, 0)
+
+        @pl.when(jnp.logical_or(zz == z, jnp.logical_not(is_end(zz))))
+        def _():
+            push(b, p_sem.at[zz], p_v, p_s)
+
         push(b, q_sem, q_v, q_s)
         to_sib(b)
 
@@ -144,10 +152,16 @@
     def from_p(zz):
         b = block(zz, p_y, p_s)
         arrived(b)
+
+        @pl.when(is_end(zz))
+        def _():
+            along(b, zz, 1)
+
+        push(b, q_sem, q_v, q_s)
         to_sib(b)
 
-    def from_q(zz):
-        b = block(zz, q_y, q_s)
+    def from_q(zz, yy, ss):
+        b = block(zz, yy, ss)
         arrived(b)
         to_sib(b)
 
@@ -210,55 +224,38 @@
         arrived(block(zz, 1, ss))
         chunk(zz, xx, k % Z == 0)
 
-    def phase1(i, carry):
-        zz = order(i)
-        arrived(block(zz, y, s))
-        line(zz)
-        from_p(order(i - 1))
-
-        @pl.when(i >= 2)
-        def _():
-            from_q(order(i - 2))
-
-        @pl.when(i == 3)
+    def turn(r, carry):
+        @pl.when(r < Z)
+        def _():
+            zz = order(r)
+            arrived(block(zz, y, s))
+            line(zz)
+
+        @pl.when(r <= Z)
+        def _():
+            from_p(order(r - 1))
+
+        @pl.when(jnp.logical_and(r >= 2, r < Z + 2))
+        def _():
+            from_q(order(r - 2), q_y, q_s)
+
+        @pl.when(r == 3)
         def _():
             load.wait()
 
-        @pl.when(i >= 3)
-        def _():
-            do_chunk(i - 3)
-
-        return carry
-
-    lax.fori_loop(1, Z, phase1, 0)
-
-    def on_to_q(zz):
-        push(block(zz, p_y, p_s), q_sem, q_v, q_s)
-
-    def early_q(i, carry):
-        on_to_q(order(i))
-        return carry
-
-    lax.fori_loop(0, Z - 1, early_q, 0)
-    from_p(order(Z - 1))
-    on_to_q(order(Z - 1))
-
-    def late_q(i, carry):
-        from_q(order(i))
-        do_chunk(i - 1)
-        return carry
-
-    lax.fori_loop(Z - 2, Z, late_q, 0)
+        @pl.when(r >= 3)
+        def _():
+            from_q(order(r - 3), 1 - y, s + flip_x)
+            do_chunk(r - 3)
+
+        @pl.when(r >= 4)
+        def _():
+            do_chunk(Z + r - 4)
+
+        return carry
+
+    lax.fori_loop(1, Z + 3, turn, 0)
     pltpu.make_async_copy(meta.at[0:n_seq - 1], meta.at[0:n_seq - 1], meta_recv).wait()
-
-    def last(i, carry):
-        b = block(order(i), 1 - y, s + flip_x)
-        arrived(b)
-        to_sib(b)
-        do_chunk(Z - 1 + i)
-        return carry
-
-    lax.fori_loop(0, Z, last, 0)
     finish(x)
     do_chunk(2 * Z - 1)
     finish(1 - x)
@@ -273,19 +270,29 @@
 
     lax.fori_loop(1, n_dev, share, 0)
 
+    def sent(sem):
+        pltpu.make_async_copy(G.at[0], G.at[0], sem).wait()
+
     def drain(zz, carry):
-        @pl.when(jnp.logical_and(zz <= z, z + 1 < Z))
-        def _():
-            pltpu.make_async_copy(G.at[0], G.at[0], up_sem.at[zz]).wait()
-
-        @pl.when(jnp.logical_and(zz >= z, z > 0))
-        def _():
-            pltpu.make_async_copy(G.at[0], G.at[0], down_sem.at[zz]).wait()
+        for side in range(2):
+            also = True if side == 0 else is_end(zz)
+
+            @pl.when(jnp.logical_and(also, jnp.logical_and(zz <= z, z + 1 < Z)))
+            def _():
+                sent(up_sem.at[side, zz])
+
+            @pl.when(jnp.logical_and(also, jnp.logical_and(zz >= z, z > 0)))
+            def _():
+                sent(down_sem.at[side, zz])
+
+        @pl.when(jnp.logical_or(zz == z, jnp.logical_not(is_end(zz))))
+        def _():
+            sent(p_sem.at[zz])
 
         return carry
 
     lax.fori_loop(0, Z, drain, 0)
-    for sem, count in ((p_sem, Z), (q_sem, 2 * Z), (sib_sem, 4 * Z)):
+    for sem, count in ((q_sem, 2 * Z), (sib_sem, 4 * Z)):
         pltpu.make_async_copy(G.at[0:count], G.at[0:count], sem).wait()
     pltpu.make_async_copy(meta.at[0:n_seq - 1], meta.at[0:n_seq - 1], meta_send).wait()
     pltpu.make_async_copy(part.at[0:n_dev - 1], part.at[0:n_dev - 1], part_recv).wait()
@@ -304,16 +311,11 @@
     ce_ref[...] = whole(loss) / count
     zr_ref[...] = jnp.sqrt(whole(keep * lse * lse) / count)
     mine = lax.broadcasted_iota(jnp.int32, (n_seq, toks), 0) == s
-    done[0] = jnp.sum(jnp.where(mine, lse, 0.0), axis=0, keepdims=True)
-    done[1] = jnp.sum(jnp.where(mine, loss, 0.0), axis=0, keepdims=True)
-    out = (
-        pltpu.make_async_copy(done.at[0], lse_ref, in_sem.at[0]),
-        pltpu.make_async_copy(done.at[1], tl_ref, in_sem.at[1]),
-    )
-    for copy in out:
-        copy.start()
-    for copy in out:
-        copy.wait()
+    done[0:1, :] = jnp.sum(jnp.where(mine, lse, 0.0), axis=0, keepdims=True)
+    done[1:2, :] = jnp.sum(jnp.where(mine, t, 0.0), axis=0, keepdims=True)
+    out = pltpu.make_async_copy(done, tok_ref, in_sem.at[0])
+    out.start()
+    out.wait()
     pltpu.make_async_copy(part.at[0:n_dev - 1], part.at[0:n_dev - 1], part_send).wait()
 
 
@@ -333,25 +335,24 @@
     dma = pltpu.SemaphoreType.DMA
     vmem = pl.BlockSpec(memory_space=pltpu.VMEM)
     hbm = pl.BlockSpec(memory_space=pltpu.HBM)
-    lse, loss, ce, root = pl.pallas_call(
+    tok, ce, root = pl.pallas_call(
         functools.partial(kernel, n_voc, n_seq),
         out_shape=(
-            jax.ShapeDtypeStruct((1, toks), f32),
-            jax.ShapeDtypeStruct((1, toks), f32),
+            jax.ShapeDtypeStruct((2, toks), f32),
             jax.ShapeDtypeStruct((1, 1), f32),
             jax.ShapeDtypeStruct((1, 1), f32),
         ),
         in_specs=[hbm, hbm, hbm, hbm],
-        out_specs=(hbm, hbm, vmem, vmem),
+        out_specs=(hbm, vmem, vmem),
         scratch_shapes=[
             pltpu.VMEM((n_dev, feat, toks), jnp.bfloat16),
             pltpu.VMEM((voc, wide), jnp.bfloat16),
             pltpu.VMEM((2, voc, 2 * toks), f32),
             pltpu.VMEM((n_seq, 8, LANES), jnp.int32),
             pltpu.VMEM((n_dev, 2 * n_seq, LANES), f32),
-            pltpu.VMEM((2, 1, toks), f32),
-            dma, dma((3,)), dma((n_dev,)), dma((n_z,)), dma((n_z,)),
-            dma, dma, dma, dma, dma, dma, dma,
+            pltpu.VMEM((2, toks), f32),
+            dma, dma((3,)), dma((n_dev,)), dma((2, n_z)), dma((2, n_z)),
+            dma((n_z,)), dma, dma, dma, dma, dma, dma,
         ],
         compiler_params=pltpu.CompilerParams(
             collective_id=0, has_side_effects=True, vmem_limit_bytes=64 * 2**20
@@ -361,7 +362,9 @@
             transcendentals=n_seq * toks * voc,
         ),
     )(hidden.T, weight, targets.reshape(1, toks), loss_mask.reshape(1, toks))
-    return (lse.reshape(toks), loss.reshape(toks), ce.reshape(()), root.reshape(()))
+    lse = tok[0]
+    loss = loss_mask.astype(f32) * (lse - tok[1])
+    return (lse, loss, ce.reshape(()), root.reshape(()))
 
 
 def solution(mesh):

time: 43.9 us -> 42.5 us (0.968)
  local copies, waits for them, and re-layouts: 2.25 us -> 0 us
  other arithmetic: 0 us -> 1.25 us
    unnamed x2 -> x0, local copies, waits for them, and re-layouts: 2.25 us -> none
    mul x0 -> x1, other arithmetic: none -> 1.25 us  [on_device(): loss = loss_mask.astype(f32) * (lse - tok[1])]
where the time goes in v3:
time: 42.5 us; the launch traced here: 42.3 us
  Pallas kernels  37 us (87%)
  between operations  4.14 us (10%)
  other arithmetic  1.25 us (3%)
    pallas_call x1, Pallas kernels, on_device(): pl.pallas_call(functools.partial(kernel, n_voc, n_seq), out_shape=(jax.Sh...  37 us
    mul x1, other arithmetic, on_device(): loss = loss_mask.astype(f32) * (lse - tok[1])  1.25 us

profile of v3, /device:TPU:0, one launch (start us, length us, event | category | flops | bytes accessed | tf_op | source)
XLA Modules:
  0.0 42.3 jit_solution(14760725913042273883)
XLA Ops:
  0.6 37.0 %shard_map.75 = (f32[2,128]{1,0:T(2,128)}, f32[1,1]{1,0:T(1,128)}, f32[1,1]{1,0:T(1,128)}) custom-call(bf16[448,128]{1,0:T(8,128)(2,1)} %bitcast.13, bf16[1000,3584]{1,0:T(8,128)(2,1)} %w_hbm.1, s32[1,128]{1,0:T(1,128)} %bitcast.14, s32[1,128]{1,0:T(1,128)} %bitcast.12), custom_call_target="tpu_custom_call" | custom-call | flops 3670016000 | bytes 7168000 | tf_op jit(solution)/shard_map/pallas_call | solution.py:338
  37.6 1.2 %fusion = (f32[128]{0:T(128)}, f32[128]{0:T(128)}) fusion(f32[2,128]{1,0:T(2,128)} %get-tuple-element.7, s32[128]{0:T(128)} %param.7), kind=kLoop, calls=%fused_computation.1 | loop fusion | flops 384 | bytes 2560 | tf_op jit(solution)/shard_map/mul | solution.py:366

commit v4 on v3

--- a/solution.py
+++ b/solution.py
@@ -56,11 +56,15 @@
     me = v * n_seq + s
     voc = w_hbm.shape[0]
     feat, toks = h_ref.shape
+    H, cut_rows = G.shape[1], G.shape[2]
 
     own = (
-        pltpu.make_async_copy(h_ref, G.at[me], in_sem.at[0]),
-        pltpu.make_async_copy(tgt_ref, meta.at[s, pl.ds(0, 1)], in_sem.at[1]),
-        pltpu.make_async_copy(msk_ref, meta.at[s, pl.ds(1, 1)], in_sem.at[2]),
+        pltpu.make_async_copy(tgt_ref, meta.at[s, pl.ds(0, 1)], in_sem.at[0]),
+        pltpu.make_async_copy(msk_ref, meta.at[s, pl.ds(1, 1)], in_sem.at[1]),
+    )
+    own += tuple(
+        pltpu.make_async_copy(h_ref.at[pl.ds(h * cut_rows, cut_rows)], G.at[me, h], in_sem.at[2 + h])
+        for h in range(H)
     )
     for copy in own:
         copy.start()
@@ -69,13 +73,26 @@
 
     barrier = pltpu.get_barrier_semaphore()
 
-    def greet(i, carry):
-        d = lax.rem(me + i, n_dev)
-        pl.semaphore_signal(barrier, inc=1, device_id=(d // n_seq, d % n_seq), device_id_type=MESH)
-        return carry
-
-    lax.fori_loop(1, n_dev, greet, 0)
-
+    def each_other(act):
+        def ring(j, carry):
+            dv = v + j
+            dv = jnp.where(dv >= n_voc, dv - n_voc, dv)
+            for k in range(1, n_seq):
+                ds = s + k
+                act(dv, jnp.where(ds >= n_seq, ds - n_seq, ds))
+
+            @pl.when(j > 0)
+            def _():
+                act(dv, s)
+
+            return carry
+
+        lax.fori_loop(0, n_voc, ring, 0)
+
+    def greet(dv, ds):
+        pl.semaphore_signal(barrier, inc=1, device_id=(dv, ds), device_id_type=MESH)
+
+    each_other(greet)
     for copy in own:
         copy.wait()
     pl.semaphore_wait(barrier, n_dev - 1)
@@ -88,15 +105,15 @@
     def block(zz, yy, ss):
         return (2 * zz + yy) * n_seq + ss
 
-    def push(b, sem, dv, ds):
+    def push(b, h, sem, dv, ds):
         pltpu.make_async_remote_copy(
-            src_ref=G.at[b], dst_ref=G.at[b], send_sem=sem, recv_sem=recv.at[b],
+            src_ref=G.at[b, h], dst_ref=G.at[b, h], send_sem=sem, recv_sem=recv.at[b, h],
             device_id=(dv, ds), device_id_type=MESH,
         ).start()
 
-    def arrived(b):
+    def arrived(b, h):
         pltpu.make_async_remote_copy(
-            src_ref=G.at[b], dst_ref=G.at[b], send_sem=sib_sem, recv_sem=recv.at[b],
+            src_ref=G.at[b, h], dst_ref=G.at[b, h], send_sem=sib_sem, recv_sem=recv.at[b, h],
             device_id=(v, sib), device_id_type=MESH,
         ).wait_recv()
 
@@ -109,33 +126,34 @@
         dist = jnp.where(in_near, (i + 1) // 2, i - near)
         return z + sgn * dist
 
-    def to_sib(b):
-        push(b, sib_sem, v, sib)
-
-    def along(b, zz, side):
+    def to_sib(b, h):
+        push(b, h, sib_sem, v, sib)
+
+    def along(b, h, zz, side):
         @pl.when(jnp.logical_and(zz <= z, z + 1 < Z))
         def _():
-            push(b, up_sem.at[side, zz], v + 2, s)
+            push(b, h, up_sem.at[side, zz, h], v + 2, s)
 
         @pl.when(jnp.logical_and(zz >= z, z > 0))
         def _():
-            push(b, down_sem.at[side, zz], v - 2, s)
+            push(b, h, down_sem.at[side, zz, h], v - 2, s)
 
     def is_end(zz):
         return jnp.logical_or(zz == 0, zz == Z - 1)
 
-    def line(zz):
+    def line(zz, h):
         b = block(zz, y, s)
-        along(b, zz, 0)
+        along(b, h, zz, 0)
 
         @pl.when(jnp.logical_or(zz == z, jnp.logical_not(is_end(zz))))
         def _():
-            push(b, p_sem.at[zz], p_v, p_s)
-
-        push(b, q_sem, q_v, q_s)
-        to_sib(b)
-
-    line(z)
+            push(b, h, p_sem.at[zz, h], p_v, p_s)
+
+        push(b, h, q_sem, q_v, q_s)
+        to_sib(b, h)
+
+    for h in range(H):
+        line(z, h)
 
     def tell(i, carry):
         d = lax.rem(s + i, n_seq)
@@ -149,40 +167,32 @@
 
     p_y, q_y = p_v % 2, q_v % 2
 
-    def from_p(zz):
+    def from_p(zz, h):
         b = block(zz, p_y, p_s)
-        arrived(b)
+        arrived(b, h)
 
         @pl.when(is_end(zz))
         def _():
-            along(b, zz, 1)
-
-        push(b, q_sem, q_v, q_s)
-        to_sib(b)
-
-    def from_q(zz, yy, ss):
+            along(b, h, zz, 1)
+
+        push(b, h, q_sem, q_v, q_s)
+        to_sib(b, h)
+
+    def from_q(zz, h, yy, ss):
         b = block(zz, yy, ss)
-        arrived(b)
-        to_sib(b)
-
-    def chunk(zz, xx, first):
+        arrived(b, h)
+        to_sib(b, h)
+
+    def chunk(zz, xx):
         sides = []
         for cc in range(2):
-            pair = [G[block(zz, yy, 2 * xx + cc)] for yy in range(2)]
+            pair = [G[block(zz, yy, 2 * xx + cc), h] for yy in range(2) for h in range(H)]
             sides.append(jnp.concatenate(pair, axis=0))
         rows = jnp.concatenate(sides, axis=1)
         cols = pl.ds(pl.multiple_of(zz * 2 * feat, LANES), 2 * feat)
-        out = lax.dot_general(
+        acc[xx] += lax.dot_general(
             W[:, cols], rows, (((1,), (0,)), ((), ())), preferred_element_type=jnp.float32
         )
-
-        @pl.when(first)
-        def _():
-            acc[xx] = out
-
-        @pl.when(jnp.logical_not(first))
-        def _():
-            acc[xx] += out
 
     step = max(r for r in range(8, 257, 8) if voc % r == 0)
 
@@ -220,74 +230,93 @@
         zz, far = order(k % Z), k // Z
         xx = x + far * (1 - 2 * x)
         ss = 2 * xx + 1 - c
-        arrived(block(zz, 0, ss))
-        arrived(block(zz, 1, ss))
-        chunk(zz, xx, k % Z == 0)
-
-    def turn(r, carry):
-        @pl.when(r < Z)
-        def _():
-            zz = order(r)
-            arrived(block(zz, y, s))
-            line(zz)
-
-        @pl.when(r <= Z)
-        def _():
-            from_p(order(r - 1))
-
-        @pl.when(jnp.logical_and(r >= 2, r < Z + 2))
-        def _():
-            from_q(order(r - 2), q_y, q_s)
-
-        @pl.when(r == 3)
+        for yy in range(2):
+            for h in range(H):
+                arrived(block(zz, yy, ss), h)
+        chunk(zz, xx)
+
+    acc[...] = jnp.zeros_like(acc)
+    items = H * Z
+
+    def turn(t, carry):
+        @pl.when(t < items)
+        def _():
+            zz, h = order(t // H), t % H
+            arrived(block(zz, y, s), h)
+            line(zz, h)
+
+        k = t - 1
+
+        @pl.when(jnp.logical_and(k >= H, k < items))
+        def _():
+            from_p(order(k // H), k % H)
+
+        j = t - 2
+
+        @pl.when(jnp.logical_and(j >= 1, j < items))
+        def _():
+            from_q(order(j // H), j % H, q_y, q_s)
+
+        i = t - 3
+
+        @pl.when(jnp.logical_and(i >= 0, i < items))
+        def _():
+            from_q(order(i // H), i % H, 1 - y, s + flip_x)
+
+        @pl.when(t == 2 * H)
         def _():
             load.wait()
 
-        @pl.when(r >= 3)
-        def _():
-            from_q(order(r - 3), 1 - y, s + flip_x)
-            do_chunk(r - 3)
-
-        @pl.when(r >= 4)
-        def _():
-            do_chunk(Z + r - 4)
+        g = t - 2 * H
+
+        @pl.when(jnp.logical_and(g >= 0, jnp.logical_and(g % H == 0, g // H < Z)))
+        def _():
+            do_chunk(g // H)
+
+        f = t - 2 * H - 1
+
+        @pl.when(jnp.logical_and(f >= 0, jnp.logical_and(f % H == 0, f // H < Z - 1)))
+        def _():
+            do_chunk(Z + f // H)
 
         return carry
 
-    lax.fori_loop(1, Z + 3, turn, 0)
+    for h in range(H):
+        from_p(z, h)
+    from_q(z, 0, q_y, q_s)
+    lax.fori_loop(H, items + 3, turn, 0)
     pltpu.make_async_copy(meta.at[0:n_seq - 1], meta.at[0:n_seq - 1], meta_recv).wait()
     finish(x)
     do_chunk(2 * Z - 1)
     finish(1 - x)
 
-    def share(i, carry):
-        d = lax.rem(me + i, n_dev)
+    def share(dv, ds):
         pltpu.make_async_remote_copy(
             src_ref=part.at[me], dst_ref=part.at[me], send_sem=part_send, recv_sem=part_recv,
-            device_id=(d // n_seq, d % n_seq), device_id_type=MESH,
+            device_id=(dv, ds), device_id_type=MESH,
         ).start()
-        return carry
-
-    lax.fori_loop(1, n_dev, share, 0)
+
+    each_other(share)
 
     def sent(sem):
-        pltpu.make_async_copy(G.at[0], G.at[0], sem).wait()
+        pltpu.make_async_copy(G.at[0, 0], G.at[0, 0], sem).wait()
 
     def drain(zz, carry):
-        for side in range(2):
-            also = True if side == 0 else is_end(zz)
-
-            @pl.when(jnp.logical_and(also, jnp.logical_and(zz <= z, z + 1 < Z)))
+        for h in range(H):
+            for side in range(2):
+                also = True if side == 0 else is_end(zz)
+
+                @pl.when(jnp.logical_and(also, jnp.logical_and(zz <= z, z + 1 < Z)))
+                def _():
+                    sent(up_sem.at[side, zz, h])
+
+                @pl.when(jnp.logical_and(also, jnp.logical_and(zz >= z, z > 0)))
+                def _():
+                    sent(down_sem.at[side, zz, h])
+
+            @pl.when(jnp.logical_or(zz == z, jnp.logical_not(is_end(zz))))
             def _():
-                sent(up_sem.at[side, zz])
-
-            @pl.when(jnp.logical_and(also, jnp.logical_and(zz >= z, z > 0)))
-            def _():
-                sent(down_sem.at[side, zz])
-
-        @pl.when(jnp.logical_or(zz == z, jnp.logical_not(is_end(zz))))
-        def _():
-            sent(p_sem.at[zz])
+                sent(p_sem.at[zz, h])
 
         return carry
 
@@ -321,11 +350,11 @@
 
 def on_device(n_voc, n_seq, hidden, weight, targets, loss_mask):
     toks, feat = hidden.shape
-    sub = 16
+    sub, pieces = 16, 2
     voc, wide = weight.shape
     fits = (
         n_seq == 4 and n_voc % 2 == 0 and n_voc >= 8 and toks == LANES
-        and feat % sub == 0 and 2 * feat % LANES == 0 and voc % 8 == 0
+        and feat % (sub * pieces) == 0 and 2 * feat % LANES == 0 and voc % 8 == 0
     )
     if not fits:
         return general(hidden, weight, targets, loss_mask)
@@ -345,14 +374,14 @@
         in_specs=[hbm, hbm, hbm, hbm],
         out_specs=(hbm, vmem, vmem),
         scratch_shapes=[
-            pltpu.VMEM((n_dev, feat, toks), jnp.bfloat16),
+            pltpu.VMEM((n_dev, pieces, feat // pieces, toks), jnp.bfloat16),
             pltpu.VMEM((voc, wide), jnp.bfloat16),
             pltpu.VMEM((2, voc, 2 * toks), f32),
             pltpu.VMEM((n_seq, 8, LANES), jnp.int32),
             pltpu.VMEM((n_dev, 2 * n_seq, LANES), f32),
             pltpu.VMEM((2, toks), f32),
-            dma, dma((3,)), dma((n_dev,)), dma((2, n_z)), dma((2, n_z)),
-            dma((n_z,)), dma, dma, dma, dma, dma, dma,
+            dma, dma((2 + pieces,)), dma((n_dev, pieces)), dma((2, n_z, pieces)), dma((2, n_z, pieces)),
+            dma((n_z, pieces)), dma, dma, dma, dma, dma, dma,
         ],
         compiler_params=pltpu.CompilerParams(
             collective_id=0, has_side_effects=True, vmem_limit_bytes=64 * 2**20

time: 42.5 us -> 43.4 us (1.021)
  Pallas kernels: 37 us -> 37.8 us
    pallas_call x1, Pallas kernels: 37 us -> 37.8 us  [on_device(): pl.pallas_call(functools.partial(kernel, n_voc, n_seq), out_shape=(jax.Sh...]
where the time goes in v4:
time: 43.4 us; the launch traced here: 43.2 us
  Pallas kernels  37.8 us (87%)
  between operations  4.14 us (10%)
  other arithmetic  1.25 us (3%)
    pallas_call x1, Pallas kernels, on_device(): pl.pallas_call(functools.partial(kernel, n_voc, n_seq), out_shape=(jax.Sh...  37.8 us
    mul x1, other arithmetic, on_device(): loss = loss_mask.astype(f32) * (lse - tok[1])  1.25 us

profile of v4, /device:TPU:0, one launch (start us, length us, event | category | flops | bytes accessed | tf_op | source)
XLA Modules:
  0.0 43.2 jit_solution(7728352007491548639)
XLA Ops:
  0.6 37.8 %shard_map.75 = (f32[2,128]{1,0:T(2,128)}, f32[1,1]{1,0:T(1,128)}, f32[1,1]{1,0:T(1,128)}) custom-call(bf16[448,128]{1,0:T(8,128)(2,1)} %bitcast.13, bf16[1000,3584]{1,0:T(8,128)(2,1)} %w_hbm.1, s32[1,128]{1,0:T(1,128)} %bitcast.14, s32[1,128]{1,0:T(1,128)} %bitcast.12), custom_call_target="tpu_custom_call" | custom-call | flops 3670016000 | bytes 7168000 | tf_op jit(solution)/shard_map/pallas_call | solution.py:367
  38.4 1.2 %fusion = (f32[128]{0:T(128)}, f32[128]{0:T(128)}) fusion(f32[2,128]{1,0:T(2,128)} %get-tuple-element.7, s32[128]{0:T(128)} %param.7), kind=kLoop, calls=%fused_computation.1 | loop fusion | flops 384 | bytes 2560 | tf_op jit(solution)/shard_map/mul | solution.py:395

commit v5 on v4

--- a/solution.py
+++ b/solution.py
@@ -46,8 +46,8 @@
     n_voc, n_seq,
     h_ref, w_hbm, tgt_ref, msk_ref,
     tok_ref, ce_ref, zr_ref,
-    G, W, acc, meta, part, done,
-    w_sem, in_sem, recv, up_sem, down_sem, p_sem, q_sem, sib_sem, meta_send, meta_recv, part_send, part_recv,
+    G, W, acc, meta, part, got, terms, done,
+    w_sem, in_sem, recv, up_sem, down_sem, p_sem, q_sem, sib_sem, meta_send, meta_recv, part_send, part_recv, term_send, term_recv,
 ):
     Z = n_voc // 2
     n_dev = n_voc * n_seq
@@ -223,8 +223,8 @@
         t = jnp.sum(t, axis=0, keepdims=True)
         for cc in range(2):
             cut = slice(cc * toks, (cc + 1) * toks)
-            part[me, pl.ds(2 * xx + cc, 1), :] = lse[:, cut]
-            part[me, pl.ds(n_seq + 2 * xx + cc, 1), :] = t[:, cut]
+            part[2 * xx + cc, 0:1, :] = lse[:, cut]
+            part[2 * xx + cc, 1:2, :] = t[:, cut]
 
     def do_chunk(k):
         zz, far = order(k % Z), k // Z
@@ -236,67 +236,60 @@
         chunk(zz, xx)
 
     acc[...] = jnp.zeros_like(acc)
-    items = H * Z
-
-    def turn(t, carry):
-        @pl.when(t < items)
-        def _():
-            zz, h = order(t // H), t % H
-            arrived(block(zz, y, s), h)
-            line(zz, h)
-
-        k = t - 1
-
-        @pl.when(jnp.logical_and(k >= H, k < items))
-        def _():
-            from_p(order(k // H), k % H)
-
-        j = t - 2
-
-        @pl.when(jnp.logical_and(j >= 1, j < items))
-        def _():
-            from_q(order(j // H), j % H, q_y, q_s)
-
-        i = t - 3
-
-        @pl.when(jnp.logical_and(i >= 0, i < items))
-        def _():
-            from_q(order(i // H), i % H, 1 - y, s + flip_x)
-
-        @pl.when(t == 2 * H)
+
+    def turn(r, carry):
+        @pl.when(r < Z)
+        def _():
+            for h in range(H):
+                arrived(block(order(r), y, s), h)
+                line(order(r), h)
+
+        @pl.when(r <= Z)
+        def _():
+            for h in range(H):
+                from_p(order(r - 1), h)
+
+        @pl.when(jnp.logical_and(r >= 2, r < Z + 2))
+        def _():
+            for h in range(H):
+                from_q(order(r - 2), h, q_y, q_s)
+
+        @pl.when(r == 3)
         def _():
             load.wait()
-
-        g = t - 2 * H
-
-        @pl.when(jnp.logical_and(g >= 0, jnp.logical_and(g % H == 0, g // H < Z)))
-        def _():
-            do_chunk(g // H)
-
-        f = t - 2 * H - 1
-
-        @pl.when(jnp.logical_and(f >= 0, jnp.logical_and(f % H == 0, f // H < Z - 1)))
-        def _():
-            do_chunk(Z + f // H)
+            pltpu.make_async_copy(meta.at[0:n_seq - 1], meta.at[0:n_seq - 1], meta_recv).wait()
+
+        @pl.when(r >= 3)
+        def _():
+            do_chunk(r - 3)
+
+        @pl.when(r == Z + 2)
+        def _():
+            finish(x)
+
+        @pl.when(r >= 3)
+        def _():
+            for h in range(H):
+                from_q(order(r - 3), h, 1 - y, s + flip_x)
+
+        @pl.when(r >= 4)
+        def _():
+            do_chunk(Z + r - 4)
 
         return carry
 
-    for h in range(H):
-        from_p(z, h)
-    from_q(z, 0, q_y, q_s)
-    lax.fori_loop(H, items + 3, turn, 0)
-    pltpu.make_async_copy(meta.at[0:n_seq - 1], meta.at[0:n_seq - 1], meta_recv).wait()
-    finish(x)
+    lax.fori_loop(1, Z + 3, turn, 0)
     do_chunk(2 * Z - 1)
     finish(1 - x)
 
     def share(dv, ds):
         pltpu.make_async_remote_copy(
-            src_ref=part.at[me], dst_ref=part.at[me], send_sem=part_send, recv_sem=part_recv,
+            src_ref=part.at[ds], dst_ref=got.at[me], send_sem=part_send, recv_sem=part_recv,
             device_id=(dv, ds), device_id_type=MESH,
         ).start()
 
     each_other(share)
+    got[me] = part[s]
 
     def sent(sem):
         pltpu.make_async_copy(G.at[0, 0], G.at[0, 0], sem).wait()
@@ -324,33 +317,44 @@
     for sem, count in ((q_sem, 2 * Z), (sib_sem, 4 * Z)):
         pltpu.make_async_copy(G.at[0:count], G.at[0:count], sem).wait()
     pltpu.make_async_copy(meta.at[0:n_seq - 1], meta.at[0:n_seq - 1], meta_send).wait()
-    pltpu.make_async_copy(part.at[0:n_dev - 1], part.at[0:n_dev - 1], part_recv).wait()
-
-    parts = part[...]
-    lses, t = parts[:, :n_seq, :], jnp.sum(parts[:, n_seq:2 * n_seq, :], axis=0)
-    top = jnp.max(lses, axis=0)
-    lse = top + jnp.log(jnp.sum(jnp.exp(lses - top[None]), axis=0))
-    keep = jnp.concatenate([meta[i, 1:2, :] for i in range(n_seq)], axis=0).astype(jnp.float32)
-    loss = keep * (lse - t)
+    pltpu.make_async_copy(got.at[0:n_dev - 1], got.at[0:n_dev - 1], part_recv).wait()
+
+    lses = got[:, 0, :]
+    t = jnp.sum(got[:, 1, :], axis=0, keepdims=True)
+    top = jnp.max(lses, axis=0, keepdims=True)
+    lse = top + jnp.log(jnp.sum(jnp.exp(lses - top), axis=0, keepdims=True))
+    mine = meta[s, 1:2, :].astype(jnp.float32)
+    terms[s, 0:1, :] = mine * (lse - t)
+    terms[s, 1:2, :] = mine * lse * lse
+
+    def pass_on(i, carry):
+        pltpu.make_async_remote_copy(
+            src_ref=terms.at[s], dst_ref=terms.at[s], send_sem=term_send, recv_sem=term_recv,
+            device_id=(v, lax.rem(s + i, n_seq)), device_id_type=MESH,
+        ).start()
+        return carry
+
+    lax.fori_loop(1, n_seq, pass_on, 0)
+    done[0:1, :] = lse
+    done[1:2, :] = t
+    out = pltpu.make_async_copy(done, tok_ref, in_sem.at[0])
+    out.start()
 
     def whole(a):
         return jnp.sum(jnp.sum(a, axis=0, keepdims=True), axis=1, keepdims=True)
 
-    count = whole(keep)
-    ce_ref[...] = whole(loss) / count
-    zr_ref[...] = jnp.sqrt(whole(keep * lse * lse) / count)
-    mine = lax.broadcasted_iota(jnp.int32, (n_seq, toks), 0) == s
-    done[0:1, :] = jnp.sum(jnp.where(mine, lse, 0.0), axis=0, keepdims=True)
-    done[1:2, :] = jnp.sum(jnp.where(mine, t, 0.0), axis=0, keepdims=True)
-    out = pltpu.make_async_copy(done, tok_ref, in_sem.at[0])
-    out.start()
+    count = whole(meta[:, 1, :].astype(jnp.float32))
+    pltpu.make_async_copy(got.at[0:n_dev - 1], got.at[0:n_dev - 1], part_send).wait()
+    pltpu.make_async_copy(terms.at[0:n_seq - 1], terms.at[0:n_seq - 1], term_recv).wait()
+    ce_ref[...] = whole(terms[:, 0, :]) / count
+    zr_ref[...] = jnp.sqrt(whole(terms[:, 1, :]) / count)
+    pltpu.make_async_copy(terms.at[0:n_seq - 1], terms.at[0:n_seq - 1], term_send).wait()
     out.wait()
-    pltpu.make_async_copy(part.at[0:n_dev - 1], part.at[0:n_dev - 1], part_send).wait()
 
 
 def on_device(n_voc, n_seq, hidden, weight, targets, loss_mask):
     toks, feat = hidden.shape
-    sub, pieces = 16, 2
+    sub, pieces = 16, 1
     voc, wide = weight.shape
     fits = (
         n_seq == 4 and n_voc % 2 == 0 and n_voc >= 8 and toks == LANES
@@ -378,10 +382,12 @@
             pltpu.VMEM((voc, wide), jnp.bfloat16),
             pltpu.VMEM((2, voc, 2 * toks), f32),
             pltpu.VMEM((n_seq, 8, LANES), jnp.int32),
-            pltpu.VMEM((n_dev, 2 * n_seq, LANES), f32),
+            pltpu.VMEM((n_seq, 2, toks), f32),
+            pltpu.VMEM((n_dev, 2, toks), f32),
+            pltpu.VMEM((n_seq, 2, toks), f32),
             pltpu.VMEM((2, toks), f32),
             dma, dma((2 + pieces,)), dma((n_dev, pieces)), dma((2, n_z, pieces)), dma((2, n_z, pieces)),
-            dma((n_z, pieces)), dma, dma, dma, dma, dma, dma,
+            dma((n_z, pieces)), dma, dma, dma, dma, dma, dma, dma, dma,
         ],
         compiler_params=pltpu.CompilerParams(
             collective_id=0, has_side_effects=True, vmem_limit_bytes=64 * 2**20

time: 43.4 us -> 43.1 us (level)
  no operation moved by 1% of the time
where the time goes in v5:
time: 43.1 us; the launch traced here: 43 us
  Pallas kernels  37.6 us (87%)
  between operations  4.14 us (10%)
  other arithmetic  1.25 us (3%)
    pallas_call x1, Pallas kernels, on_device(): pl.pallas_call(functools.partial(kernel, n_voc, n_seq), out_shape=(jax.Sh...  37.6 us
    mul x1, other arithmetic, on_device(): loss = loss_mask.astype(f32) * (lse - tok[1])  1.25 us

profile of v5, /device:TPU:0, one launch (start us, length us, event | category | flops | bytes accessed | tf_op | source)
XLA Modules:
  0.0 43.0 jit_solution(16202866749410655865)
XLA Ops:
  0.6 37.6 %shard_map.75 = (f32[2,128]{1,0:T(2,128)}, f32[1,1]{1,0:T(1,128)}, f32[1,1]{1,0:T(1,128)}) custom-call(bf16[448,128]{1,0:T(8,128)(2,1)} %bitcast.13, bf16[1000,3584]{1,0:T(8,128)(2,1)} %w_hbm.1, s32[1,128]{1,0:T(1,128)} %bitcast.14, s32[1,128]{1,0:T(1,128)} %bitcast.12), custom_call_target="tpu_custom_call" | custom-call | flops 3670016000 | bytes 7168000 | tf_op jit(solution)/shard_map/pallas_call | solution.py:371
  38.2 1.2 %fusion = (f32[128]{0:T(128)}, f32[128]{0:T(128)}) fusion(f32[2,128]{1,0:T(2,128)} %get-tuple-element.7, s32[128]{0:T(128)} %param.7), kind=kLoop, calls=%fused_computation.1 | loop fusion | flops 384 | bytes 2560 | tf_op jit(solution)/shard_map/mul | solution.py:401

commit v6 on v3

--- a/solution.py
+++ b/solution.py
@@ -121,14 +121,14 @@
         def _():
             push(b, down_sem.at[side, zz], v - 2, s)
 
-    def is_end(zz):
-        return jnp.logical_or(zz == 0, zz == Z - 1)
+    def by_z(zz):
+        return zz != Z // 2
 
     def line(zz):
         b = block(zz, y, s)
         along(b, zz, 0)
 
-        @pl.when(jnp.logical_or(zz == z, jnp.logical_not(is_end(zz))))
+        @pl.when(jnp.logical_or(zz == z, jnp.logical_not(by_z(zz))))
         def _():
             push(b, p_sem.at[zz], p_v, p_s)
 
@@ -153,7 +153,7 @@
         b = block(zz, p_y, p_s)
         arrived(b)
 
-        @pl.when(is_end(zz))
+        @pl.when(by_z(zz))
         def _():
             along(b, zz, 1)
 
@@ -275,7 +275,7 @@
 
     def drain(zz, carry):
         for side in range(2):
-            also = True if side == 0 else is_end(zz)
+            also = True if side == 0 else by_z(zz)
 
             @pl.when(jnp.logical_and(also, jnp.logical_and(zz <= z, z + 1 < Z)))
             def _():
@@ -285,7 +285,7 @@
             def _():
                 sent(down_sem.at[side, zz])
 
-        @pl.when(jnp.logical_or(zz == z, jnp.logical_not(is_end(zz))))
+        @pl.when(jnp.logical_or(zz == z, jnp.logical_not(by_z(zz))))
         def _():
             sent(p_sem.at[zz])
 

time: 42.5 us -> 46.3 us (1.089)
  Pallas kernels: 37 us -> 40.7 us
    pallas_call x1, Pallas kernels: 37 us -> 40.7 us  [on_device(): pl.pallas_call(functools.partial(kernel, n_voc, n_seq), out_shape=(jax.Sh...]
where the time goes in v6:
time: 46.3 us; the launch traced here: 46.1 us
  Pallas kernels  40.7 us (88%)
  between operations  4.14 us (9%)
  other arithmetic  1.25 us (3%)
    pallas_call x1, Pallas kernels, on_device(): pl.pallas_call(functools.partial(kernel, n_voc, n_seq), out_shape=(jax.Sh...  40.7 us
    mul x1, other arithmetic, on_device(): loss = loss_mask.astype(f32) * (lse - tok[1])  1.25 us

profile of v6, /device:TPU:0, one launch (start us, length us, event | category | flops | bytes accessed | tf_op | source)
XLA Modules:
  0.0 46.1 jit_solution(15379638731151777158)
XLA Ops:
  0.6 40.7 %shard_map.75 = (f32[2,128]{1,0:T(2,128)}, f32[1,1]{1,0:T(1,128)}, f32[1,1]{1,0:T(1,128)}) custom-call(bf16[448,128]{1,0:T(8,128)(2,1)} %bitcast.13, bf16[1000,3584]{1,0:T(8,128)(2,1)} %w_hbm.1, s32[1,128]{1,0:T(1,128)} %bitcast.14, s32[1,128]{1,0:T(1,128)} %bitcast.12), custom_call_target="tpu_custom_call" | custom-call | flops 3670016000 | bytes 7168000 | tf_op jit(solution)/shard_map/pallas_call | solution.py:338
  41.3 1.2 %fusion = (f32[128]{0:T(128)}, f32[128]{0:T(128)}) fusion(f32[2,128]{1,0:T(2,128)} %get-tuple-element.7, s32[128]{0:T(128)} %param.7), kind=kLoop, calls=%fused_computation.1 | loop fusion | flops 384 | bytes 2560 | tf_op jit(solution)/shard_map/mul | solution.py:366

commit v7 on v6

--- a/solution.py
+++ b/solution.py
@@ -112,26 +112,19 @@
     def to_sib(b):
         push(b, sib_sem, v, sib)
 
-    def along(b, zz, side):
+    def along(b, zz):
         @pl.when(jnp.logical_and(zz <= z, z + 1 < Z))
         def _():
-            push(b, up_sem.at[side, zz], v + 2, s)
+            push(b, up_sem.at[zz], v + 2, s)
 
         @pl.when(jnp.logical_and(zz >= z, z > 0))
         def _():
-            push(b, down_sem.at[side, zz], v - 2, s)
-
-    def by_z(zz):
-        return zz != Z // 2
+            push(b, down_sem.at[zz], v - 2, s)
 
     def line(zz):
         b = block(zz, y, s)
-        along(b, zz, 0)
-
-        @pl.when(jnp.logical_or(zz == z, jnp.logical_not(by_z(zz))))
-        def _():
-            push(b, p_sem.at[zz], p_v, p_s)
-
+        along(b, zz)
+        push(b, p_sem.at[zz], p_v, p_s)
         push(b, q_sem, q_v, q_s)
         to_sib(b)
 
@@ -152,11 +145,6 @@
     def from_p(zz):
         b = block(zz, p_y, p_s)
         arrived(b)
-
-        @pl.when(by_z(zz))
-        def _():
-            along(b, zz, 1)
-
         push(b, q_sem, q_v, q_s)
         to_sib(b)
 
@@ -274,21 +262,15 @@
         pltpu.make_async_copy(G.at[0], G.at[0], sem).wait()
 
     def drain(zz, carry):
-        for side in range(2):
-            also = True if side == 0 else by_z(zz)
-
-            @pl.when(jnp.logical_and(also, jnp.logical_and(zz <= z, z + 1 < Z)))
-            def _():
-                sent(up_sem.at[side, zz])
-
-            @pl.when(jnp.logical_and(also, jnp.logical_and(zz >= z, z > 0)))
-            def _():
-                sent(down_sem.at[side, zz])
-
-        @pl.when(jnp.logical_or(zz == z, jnp.logical_not(by_z(zz))))
-        def _():
-            sent(p_sem.at[zz])
-
+        @pl.when(jnp.logical_and(zz <= z, z + 1 < Z))
+        def _():
+            sent(up_sem.at[zz])
+
+        @pl.when(jnp.logical_and(zz >= z, z > 0))
+        def _():
+            sent(down_sem.at[zz])
+
+        sent(p_sem.at[zz])
         return carry
 
     lax.fori_loop(0, Z, drain, 0)
@@ -351,7 +333,7 @@
             pltpu.VMEM((n_seq, 8, LANES), jnp.int32),
             pltpu.VMEM((n_dev, 2 * n_seq, LANES), f32),
             pltpu.VMEM((2, toks), f32),
-            dma, dma((3,)), dma((n_dev,)), dma((2, n_z)), dma((2, n_z)),
+            dma, dma((3,)), dma((n_dev,)), dma((n_z,)), dma((n_z,)),
             dma((n_z,)), dma, dma, dma, dma, dma, dma,
         ],
         compiler_params=pltpu.CompilerParams(

time: 46.3 us -> 43.1 us (0.931)
  Pallas kernels: 40.7 us -> 37.5 us
    pallas_call x1, Pallas kernels: 40.7 us -> 37.5 us  [on_device(): pl.pallas_call(functools.partial(kernel, n_voc, n_seq), out_shape=(jax.Sh...]
where the time goes in v7:
time: 43.1 us; the launch traced here: 42.9 us
  Pallas kernels  37.5 us (87%)
  between operations  4.14 us (10%)
  other arithmetic  1.25 us (3%)
    pallas_call x1, Pallas kernels, on_device(): pl.pallas_call(functools.partial(kernel, n_voc, n_seq), out_shape=(jax.Sh...  37.5 us
    mul x1, other arithmetic, on_device(): loss = loss_mask.astype(f32) * (lse - tok[1])  1.25 us

profile of v7, /device:TPU:0, one launch (start us, length us, event | category | flops | bytes accessed | tf_op | source)
XLA Modules:
  0.0 42.9 jit_solution(13460805829848822123)
XLA Ops:
  0.6 37.5 %shard_map.75 = (f32[2,128]{1,0:T(2,128)}, f32[1,1]{1,0:T(1,128)}, f32[1,1]{1,0:T(1,128)}) custom-call(bf16[448,128]{1,0:T(8,128)(2,1)} %bitcast.13, bf16[1000,3584]{1,0:T(8,128)(2,1)} %w_hbm.1, s32[1,128]{1,0:T(1,128)} %bitcast.14, s32[1,128]{1,0:T(1,128)} %bitcast.12), custom_call_target="tpu_custom_call" | custom-call | flops 3670016000 | bytes 7168000 | tf_op jit(solution)/shard_map/pallas_call | solution.py:320
  38.1 1.2 %fusion = (f32[128]{0:T(128)}, f32[128]{0:T(128)}) fusion(f32[2,128]{1,0:T(2,128)} %get-tuple-element.7, s32[128]{0:T(128)} %param.7), kind=kLoop, calls=%fused_computation.1 | loop fusion | flops 384 | bytes 2560 | tf_op jit(solution)/shard_map/mul | solution.py:348
